TPU v7x, 256 devices: a whole 4x4x8 slice. The times are simulated.
256 devices in a mesh: chain: 32 (over z, x), sector: 8 (over y, core).
Axes of the slice: x: 4, y: 4, z: 8, core: 2. Of those that a mesh axis runs over, the one named last changes fastest.
Arguments:
- left_env: bfloat16 [32, 8, 14, 256, 256], P('chain', 'sector'), may hold values from -6 to 6
- right_env: bfloat16 [32, 8, 14, 256, 256], P('chain', 'sector'), may hold values from -6 to 6
- left_state: bfloat16 [32, 8, 4, 256, 256], P('chain', 'sector'), may hold values from -0.375 to 0.375
- right_state: bfloat16 [32, 8, 4, 256, 256], P('chain', 'sector'), may hold values from -0.375 to 0.375
- mpo: bfloat16 [14, 4, 4, 14], replicated, may hold values from -1.5 to 1.5
- couple: int32 [32, 4, 8], P('chain', None, 'sector'), may hold values 0 or 1
- sizes: int32 [8], replicated, may hold values from 1 to 256, 1536 in all
Outputs:
- left_out: bfloat16 [32, 8, 14, 256, 256], P('chain', 'sector')
- right_out: bfloat16 [32, 8, 14, 256, 256], P('chain', 'sector')
Inputs may be any that keep to these rules, and one draw needn't show every extreme that they name: The 8 sizes sum to 1536.
All inputs are finite; a program needn't handle non-finite values. No bound on the sum of `couple` on one device may be relied on, other than what follows from the above.
Results may differ from a plain program's by a relative error of at most 0.0057.
Values may be sent and summed in bfloat16 or wider, within the bound.
A program may use at most 128 MiB of HBM per device.

v0:
```python
import jax
import jax.numpy as jnp
from jax import lax
from jax.sharding import PartitionSpec as P

OFFSETS = (0, 1, 1, 2)
GROUPS = ((0,), (1, 2), (3,))


def from_behind(value, axis, steps):
    count = lax.axis_size(axis)
    initial, last = (max(0, -steps), min(count, count - steps))
    return lax.ppermute(value, axis, [(source, source + steps) for source in range(initial, last)])


def masked_site(site_tensor, couple_col, sizes, sector_pos):
    slot_size = site_tensor.shape[1]
    row_ids = jnp.arange(slot_size, dtype=jnp.int32)
    columns_live = sizes[sector_pos]
    pieces_list = []
    for physical in range(4):
        source_pos = sector_pos - OFFSETS[physical]
        live_rows = jnp.where(source_pos >= 0, sizes[jnp.maximum(source_pos, 0)], 0)
        keep_mask = (
            (row_ids[:, None] < live_rows)
            & (row_ids[None, :] < columns_live)
            & (couple_col[physical] > 0)
        )
        pieces_list.append(
            jnp.where(keep_mask, site_tensor[physical], jnp.zeros_like(site_tensor[physical]))
        )
    return jnp.stack(pieces_list)


def left_mixer(weights, members):
    picked = weights[:, list(members)][:, :, list(members)]
    group_size = len(members)
    mpo_width = weights.shape[0]
    return jnp.transpose(picked, (3, 1, 2, 0)).reshape(
        mpo_width * group_size, group_size * mpo_width
    )


def right_mixer(weights, members):
    picked = weights[:, list(members)][:, :, list(members)]
    group_size = len(members)
    mpo_width = weights.shape[0]
    return picked.reshape(mpo_width * group_size, group_size * mpo_width)


def left_group(env_src, site_m, weights, members):
    mpo_width, slot_size = (env_src.shape[0], env_src.shape[1])
    flattened = env_src.reshape(mpo_width * slot_size, slot_size)
    products = []
    for physical in members:
        operand = site_m[physical]
        products.append(
            (
                lambda operand=operand: jnp.dot(
                    flattened, operand, preferred_element_type=jnp.float32
                ).astype(jnp.bfloat16)
            )()
        )
    group_size = len(members)
    stacked = jnp.stack(products).reshape(group_size * mpo_width, slot_size * slot_size)
    mixed_terms = jnp.dot(left_mixer(weights, members), stacked, preferred_element_type=jnp.float32)
    mixed_terms = mixed_terms.astype(jnp.bfloat16).reshape(
        mpo_width, group_size, slot_size, slot_size
    )
    chosen = site_m[members[0] : members[-1] + 1]
    return jnp.einsum("sab,vsac->vbc", chosen, mixed_terms, preferred_element_type=jnp.float32)


def right_group(env_blk, site_m, weights, members):
    mpo_width, slot_size = (env_blk.shape[0], env_blk.shape[1])
    flattened = env_blk.reshape(mpo_width * slot_size, slot_size)
    products = []
    for physical in members:
        operand = site_m[physical]
        products.append(
            (
                lambda operand=operand: lax.dot_general(
                    flattened, operand, (((1,), (1,)), ((), ())), preferred_element_type=jnp.float32
                ).astype(jnp.bfloat16)
            )()
        )
    group_size = len(members)
    stacked = jnp.stack(products).reshape(group_size * mpo_width, slot_size * slot_size)
    mixed_terms = jnp.dot(
        right_mixer(weights, members), stacked, preferred_element_type=jnp.float32
    )
    mixed_terms = mixed_terms.astype(jnp.bfloat16).reshape(
        mpo_width, group_size, slot_size, slot_size
    )
    chosen = site_m[members[0] : members[-1] + 1]
    return jnp.einsum("sab,wsbc->wac", chosen, mixed_terms, preferred_element_type=jnp.float32)


def body(left_env, right_env, left_state, right_state, mpo, couple, sizes):
    chain_pos = lax.axis_index("chain")
    sector_pos = lax.axis_index("sector")
    sector_count = lax.axis_size("sector")
    chain_count = lax.axis_size("chain")
    left_site_m = masked_site(left_state[0, 0], couple[0, :, 0], sizes, sector_pos)
    right_site_m = masked_site(right_state[0, 0], couple[0, :, 0], sizes, sector_pos)
    own_env = left_env[0, 0]
    lower_envs = [own_env]
    for distance in (1, 2):
        lower_envs.append(from_behind(own_env, "sector", distance))
    summed = jnp.zeros(own_env.shape, jnp.float32)
    for members in GROUPS:
        summed = summed + left_group(lower_envs[OFFSETS[members[0]]], left_site_m, mpo, members)
    passed_env = from_behind(summed.astype(jnp.bfloat16), "chain", 1)
    left_out = jnp.where(chain_pos == 0, own_env, passed_env)
    right_block = right_env[0, 0]
    right_sum = jnp.zeros(right_block.shape, jnp.float32)
    for group_pos in range(3):
        partial_sum = right_group(right_block, right_site_m, mpo, GROUPS[group_pos])
        received = from_behind(partial_sum, ("chain", "sector"), -(sector_count + group_pos))
        right_sum = right_sum + jnp.where(
            sector_pos + group_pos < sector_count, received, jnp.zeros_like(received)
        )
    right_out = jnp.where(chain_pos == chain_count - 1, right_block, right_sum.astype(jnp.bfloat16))
    return (left_out[None, None], right_out[None, None])


def solution(mesh):
    placed = (
        P("chain", "sector", None, None, None),
        P("chain", "sector", None, None, None),
        P("chain", "sector", None, None, None),
        P("chain", "sector", None, None, None),
        P(),
        P("chain", None, "sector"),
        P(),
    )
    return jax.shard_map(
        body,
        mesh=mesh,
        in_specs=placed,
        out_specs=(P("chain", "sector", None, None, None), P("chain", "sector", None, None, None)),
        check_vma=False,
    )
```

profile of v0, /device:TPU:39, one launch (start us, length us, event | category | flops | bytes accessed | tf_op | source)
XLA Modules:
  0.0 309.1 jit_solution(17309891391753796323)
XLA Ops:
  0.7 4.0 %copy.55 = bf16[1,1,14,256,256]{3,4,2,1,0:T(8,128)(2,1)} copy(bf16[1,1,14,256,256]{4,3,2,1,0:T(8,128)(2,1)} %param.19) | data formatting | bytes 3670016 | tf_op args[0]
  4.6 3.8 %collective-permute-start = (bf16[14,256,256]{1,2,0:T(8,128)(2,1)}, bf16[14,256,256]{1,2,0:T(8,128)(2,1)}, u32[]{:S(2)}, u32[]{:S(2)}) collective-permute-start(bf16[14,256,256]{1,2,0:T(8,128)(2,1)} %bitcast.201), channel_id=1, source_target_pairs={{0,1},{1,2},{2,3},{3,4},{4,5},{5,6},{6,7},{8,9},{9,10},{10,11},{11... | collective-permute-start | bytes 5505032 | tf_op jit(solution)/shard_map/ppermute | solution.py:13
  8.4 4.5 %collective-permute-start.1 = (bf16[14,256,256]{1,2,0:T(8,128)(2,1)}, bf16[14,256,256]{1,2,0:T(8,128)(2,1)}, u32[]{:S(2)}, u32[]{:S(2)}) collective-permute-start(bf16[14,256,256]{1,2,0:T(8,128)(2,1)} %bitcast.202), channel_id=1, source_target_pairs={{0,2},{1,3},{2,4},{3,5},{4,6},{5,7},{8,10},{9,11},{10,12},{11,13},... | collective-permute-start | bytes 5505032 | tf_op jit(solution)/shard_map/ppermute | solution.py:13
  18.2 2.1 pad_maximum_fusion.1
  20.3 5.9 %copy.73 = bf16[2,3584,256]{2,1,0:T(8,128)(2,1)} copy(bf16[2,3584,256]{1,2,0:T(8,128)(2,1)} %pad_maximum_fusion.1) | data formatting | bytes 7340032 | tf_op jit(solution)/shard_map/stack | solution.py:88
  26.3 5.7 %reshape.686 = bf16[28,65536]{1,0:T(8,128)(2,1)} reshape(bf16[2,3584,256]{2,1,0:T(8,128)(2,1)} %copy.73) | data formatting | bytes 7340032 | tf_op jit(solution)/shard_map/reshape | solution.py:88
  33.3 3.4 %convolution_convert_fusion = bf16[28,65536]{1,0:T(8,128)(2,1)S(1)} fusion(bf16[28,28]{1,0:T(8,128)(2,1)S(1)} %reshape.685, bf16[28,65536]{1,0:T(8,128)(2,1)} %reshape.686), kind=kOutput, calls=%fused_computation.2 | convolution fusion | flops 104595456 | bytes 7341600 | tf_op jit(solution)/shard_map/dot_general | solution.py:89
  39.0 3.1 convolution_bitcast_fusion.1
  42.1 1.9 collective-permute-start.4
  45.3 1.9 fusion.7
  47.2 3.8 %copy.75 = bf16[3584,256]{1,0:T(8,128)(2,1)} copy(bf16[3584,256]{0,1:T(8,128)(2,1)} %fusion.7) | data formatting | bytes 3670016 | tf_op jit(solution)/shard_map/convert_element_type | solution.py:84
  51.1 3.2 %reshape_stack.15 = bf16[14,65536]{1,0:T(8,128)(2,1)} reshape(bf16[3584,256]{1,0:T(8,128)(2,1)} %copy.75) | data formatting | bytes 3670016 | tf_op jit(solution)/shard_map/reshape;stack | solution.py:88
  54.2 2.3 convolution_convert_fusion.2
  57.0 2.6 convolution_bitcast_fusion
  59.6 2.1 collective-permute-start.5
  63.0 1.9 fusion.4
  64.9 3.8 %copy.69 = bf16[3584,256]{1,0:T(8,128)(2,1)} copy(bf16[3584,256]{0,1:T(8,128)(2,1)} %fusion.4) | data formatting | bytes 3670016 | tf_op jit(solution)/shard_map/convert_element_type | solution.py:84
  68.7 3.2 %reshape_stack.14 = bf16[14,65536]{1,0:T(8,128)(2,1)} reshape(bf16[3584,256]{1,0:T(8,128)(2,1)} %copy.69) | data formatting | bytes 3670016 | tf_op jit(solution)/shard_map/reshape;stack | solution.py:88
  71.9 2.3 convolution_convert_fusion.3
  74.6 2.6 convolution_bitcast_fusion.2
  77.3 2.7 collective-permute-start.3
  80.1 3.5 %fusion = bf16[3584,256]{0,1:T(8,128)(2,1)} fusion(bf16[3584,256]{1,0:T(8,128)(2,1)} %bitcast.199, bf16[1,1,4,256,256]{4,3,2,1,0:T(8,128)(2,1)S(1)} %copy-done.5, pred[]{:T(512)} %bitcast.3, pred[256]{0:T(512)(128)(4,1)S(1)} %iota_compare_fusion.2, pred[256]{0:T(512)(128)(4,1)S(1)} %iota_compare_fusion.3), kind=kOutput, calls=%fused_computation.16 | convolution fusion | flops 470876160 | bytes 3802113 | tf_op jit(solution)/shard_map/dot_general | solution.py:59
  83.6 3.8 %copy.56 = bf16[3584,256]{1,0:T(8,128)(2,1)} copy(bf16[3584,256]{0,1:T(8,128)(2,1)} %fusion) | data formatting | bytes 3670016 | tf_op jit(solution)/shard_map/convert_element_type | solution.py:61
  87.4 3.2 %reshape_stack.12 = bf16[14,65536]{1,0:T(8,128)(2,1)} reshape(bf16[3584,256]{1,0:T(8,128)(2,1)} %copy.56) | data formatting | bytes 3670016 | tf_op jit(solution)/shard_map/reshape;stack | solution.py:65
  90.6 3.6 %convolution_convert_fusion.5 = bf16[65536,14]{0,1:T(8,128)(2,1)} fusion(bf16[14,65536]{1,0:T(8,128)(2,1)} %reshape_stack.12, bf16[14,1,1,14]{0,3,2,1:T(8,128)(2,1)S(1)} %copy.88), kind=kOutput, calls=%fused_computation.7 | convolution fusion | flops 26607616 | bytes 3670408 | tf_op jit(solution)/shard_map/dot_general | solution.py:66
  94.5 2.1 copy.92
  96.6 2.6 fusion.15
  99.2 3.8 %copy.61 = bf16[14,256,256]{2,1,0:T(8,128)(2,1)} copy(bf16[14,256,256]{1,2,0:T(8,128)(2,1)} %collective-permute-done) | data formatting | bytes 3670016 | tf_op jit(solution)/shard_map/ppermute | solution.py:13
  103.0 2.4 fusion.1
  106.3 2.1 pad_maximum_fusion
  108.4 6.0 %copy.62 = bf16[2,3584,256]{2,1,0:T(8,128)(2,1)} copy(bf16[2,3584,256]{1,2,0:T(8,128)(2,1)} %pad_maximum_fusion) | data formatting | bytes 7340032 | tf_op jit(solution)/shard_map/stack | solution.py:65
  114.3 5.7 %reshape.678 = bf16[28,65536]{1,0:T(8,128)(2,1)} reshape(bf16[2,3584,256]{2,1,0:T(8,128)(2,1)} %copy.62) | data formatting | bytes 7340032 | tf_op jit(solution)/shard_map/reshape | solution.py:65
  120.0 3.4 %convolution_convert_fusion.1 = bf16[28,65536]{1,0:T(8,128)(2,1)S(1)} fusion(bf16[28,28]{1,0:T(8,128)(2,1)S(1)} %reshape.676, bf16[28,65536]{1,0:T(8,128)(2,1)} %reshape.678), kind=kOutput, calls=%fused_computation.3 | convolution fusion | flops 104595456 | bytes 7341600 | tf_op jit(solution)/shard_map/dot_general | solution.py:66
  124.4 2.0 slice.119
  126.4 3.8 %copy.64 = bf16[14,256,256]{2,1,0:T(8,128)(2,1)} copy(bf16[14,256,256]{1,2,0:T(8,128)(2,1)} %collective-permute-done.1) | data formatting | bytes 3670016 | tf_op jit(solution)/shard_map/ppermute | solution.py:13
  130.2 3.5 %fusion.3 = bf16[3584,256]{0,1:T(8,128)(2,1)} fusion(bf16[3584,256]{1,0:T(8,128)(2,1)} %bitcast.200, bf16[1,1,4,256,256]{4,3,2,1,0:T(8,128)(2,1)S(1)} %copy-done.5, pred[]{:T(512)} %bitcast.29, pred[256]{0:T(512)(128)(4,1)S(1)} %iota_compare_fusion.2, pred[256]{0:T(512)(128)(4,1)S(1)} %iota_compare_fusion), kind=kOutput, calls=%fused_computation.19 | convolution fusion | flops 470876160 | bytes 3802113 | tf_op jit(solution)/shard_map/dot_general | solution.py:59
  133.7 3.8 %copy.65 = bf16[3584,256]{1,0:T(8,128)(2,1)} copy(bf16[3584,256]{0,1:T(8,128)(2,1)} %fusion.3) | data formatting | bytes 3670016 | tf_op jit(solution)/shard_map/convert_element_type | solution.py:61
  137.5 3.2 %reshape_stack.13 = bf16[14,65536]{1,0:T(8,128)(2,1)} reshape(bf16[3584,256]{1,0:T(8,128)(2,1)} %copy.65) | data formatting | bytes 3670016 | tf_op jit(solution)/shard_map/reshape;stack | solution.py:65
  140.7 2.3 convolution_convert_fusion.4
  147.1 2.0 fusion.17
  149.1 4.7 %collective-permute-start.2 = (bf16[14,256,256]{1,2,0:T(8,128)(2,1)}, bf16[14,256,256]{1,2,0:T(8,128)(2,1)}, u32[]{:S(2)}, u32[]{:S(2)}) collective-permute-start(bf16[14,256,256]{1,2,0:T(8,128)(2,1)} %fusion.17), channel_id=1, source_target_pairs={{0,8},{8,16},{16,24},{24,32},{32,40},{40,48},{48,56},{56,64},{64,7... | collective-permute-start | bytes 5505032 | tf_op jit(solution)/shard_map/ppermute | solution.py:13
  153.7 2.6 copy.68
  156.3 46.1 %collective-permute-done.5 = f32[14,256,256]{1,2,0:T(8,128)} collective-permute-done((f32[14,256,256]{1,2,0:T(8,128)}, f32[14,256,256]{1,2,0:T(8,128)}, u32[]{:S(2)}, u32[]{:S(2)}) %collective-permute-start.5) | collective-permute-done | bytes 3670048 | tf_op jit(solution)/shard_map/ppermute | solution.py:13
  202.4 88.9 %collective-permute-done.3 = f32[14,256,256]{1,2,0:T(8,128)} collective-permute-done((f32[14,256,256]{1,2,0:T(8,128)}, f32[14,256,256]{1,2,0:T(8,128)}, u32[]{:S(2)}, u32[]{:S(2)}) %collective-permute-start.3) | collective-permute-done | bytes 3670048 | tf_op jit(solution)/shard_map/ppermute | solution.py:13
  291.2 7.2 %fusion.11 = bf16[1,1,14,256,256]{3,4,2,1,0:T(8,128)(2,1)} fusion(f32[14,256,256]{1,2,0:T(8,128)} %collective-permute-done.5, f32[14,256,256]{1,2,0:T(8,128)} %collective-permute-done.4, f32[14,256,256]{1,2,0:T(8,128)} %collective-permute-done.3, bf16[1,1,14,256,256]{3,4,2,1,0:T(8,128)(2,1)} %copy.68, pred[]{:T(512)S(6)} %lt.146, pred[]{:T(512)S(6)} %lt.143, ...), kind=kLoop, calls=%fused_computation.34 | loop fusion | flops 6422528 | bytes 14680068 | tf_op jit(solution)/shard_map/broadcast_in_dim | solution.py:124
  298.5 3.9 %copy.79 = bf16[1,1,14,256,256]{4,3,2,1,0:T(8,128)(2,1)} copy(bf16[1,1,14,256,256]{3,4,2,1,0:T(8,128)(2,1)} %fusion.11) | data formatting | bytes 3670016
  302.4 2.9 select_bitcast_fusion
  305.3 3.8 %copy.78 = bf16[1,1,14,256,256]{4,3,2,1,0:T(8,128)(2,1)} copy(bf16[1,1,14,256,256]{3,4,2,1,0:T(8,128)(2,1)} %select_bitcast_fusion) | data formatting | bytes 3670016
  (54 shorter events, 14.1 us)
Async XLA Ops:
  0.6 12.2 %copy-start.8 = (s32[8]{0:T(128)S(1)}, s32[8]{0:T(128)}, u32[]{:S(2)}) copy-start(s32[8]{0:T(128)} %param.25) | copy-start | bytes 100
  0.6 14.2 %copy-start.9 = (s32[1,4,1]{1,2,0:T(1,128)S(1)}, s32[1,4,1]{1,2,0:T(1,128)}, u32[]{:S(2)}) copy-start(s32[1,4,1]{1,2,0:T(1,128)} %param.24) | copy-start | bytes 52
  0.7 16.2 %copy-start = (bf16[1,1,14,256,256]{4,3,2,1,0:T(8,128)(2,1)S(1)}, bf16[1,1,14,256,256]{4,3,2,1,0:T(8,128)(2,1)}, u32[]{:S(2)}) copy-start(bf16[1,1,14,256,256]{4,3,2,1,0:T(8,128)(2,1)} %param.20) | copy-start | bytes 5505028
  0.7 16.2 %copy-start.6 = (bf16[1,1,4,256,256]{4,3,2,1,0:T(8,128)(2,1)S(1)}, bf16[1,1,4,256,256]{4,3,2,1,0:T(8,128)(2,1)}, u32[]{:S(2)}) copy-start(bf16[1,1,4,256,256]{4,3,2,1,0:T(8,128)(2,1)} %param.22) | copy-start | bytes 1572868
  4.6 94.6 %collective-permute-start = (bf16[14,256,256]{1,2,0:T(8,128)(2,1)}, bf16[14,256,256]{1,2,0:T(8,128)(2,1)}, u32[]{:S(2)}, u32[]{:S(2)}) collective-permute-start(bf16[14,256,256]{1,2,0:T(8,128)(2,1)} %bitcast.201), channel_id=1, source_target_pairs={{0,1},{1,2},{2,3},{3,4},{4,5},{5,6},{6,7},{8,9},{9,10},{10,11},{11... | collective-permute-start | bytes 5505032 | tf_op jit(solution)/shard_map/ppermute | solution.py:13
  8.4 118.0 %collective-permute-start.1 = (bf16[14,256,256]{1,2,0:T(8,128)(2,1)}, bf16[14,256,256]{1,2,0:T(8,128)(2,1)}, u32[]{:S(2)}, u32[]{:S(2)}) collective-permute-start(bf16[14,256,256]{1,2,0:T(8,128)(2,1)} %bitcast.202), channel_id=1, source_target_pairs={{0,2},{1,3},{2,4},{3,5},{4,6},{5,7},{8,10},{9,11},{10,12},{11,13},... | collective-permute-start | bytes 5505032 | tf_op jit(solution)/shard_map/ppermute | solution.py:13
  26.3 5.7 %copy-start.10 = (s32[2]{0:T(128)S(1)}, s32[2]{0:T(128)}, u32[]{:S(2)}) copy-start(s32[2]{0:T(128)} %constant.144) | copy-start | bytes 28
  26.3 5.7 %copy-start.7 = (bf16[14,4,4,14]{3,2,1,0:T(4,128)(2,1)S(1)}, bf16[14,4,4,14]{3,2,1,0:T(4,128)(2,1)}, u32[]{:S(2)}) copy-start(bf16[14,4,4,14]{3,2,1,0:T(4,128)(2,1)} %param.23) | copy-start | bytes 18820
  37.7 1.0 copy-start.5
  42.1 114.2 %collective-permute-start.4 = (f32[14,256,256]{1,2,0:T(8,128)}, f32[14,256,256]{1,2,0:T(8,128)}, u32[]{:S(2)}, u32[]{:S(2)}) collective-permute-start(f32[14,256,256]{1,2,0:T(8,128)} %convolution_bitcast_fusion.1), channel_id=1, source_target_pairs={{9,0},{10,1},{11,2},{12,3},{13,4},{14,5},{15,6},{16,7},{17,8},{18,... | collective-permute-start | bytes 11010056 | tf_op jit(solution)/shard_map/ppermute | solution.py:13
  59.6 142.8 %collective-permute-start.5 = (f32[14,256,256]{1,2,0:T(8,128)}, f32[14,256,256]{1,2,0:T(8,128)}, u32[]{:S(2)}, u32[]{:S(2)}) collective-permute-start(f32[14,256,256]{1,2,0:T(8,128)} %convolution_bitcast_fusion), channel_id=1, source_target_pairs={{10,0},{11,1},{12,2},{13,3},{14,4},{15,5},{16,6},{17,7},{18,8},{19... | collective-permute-start | bytes 11010056 | tf_op jit(solution)/shard_map/ppermute | solution.py:13
  77.3 214.0 %collective-permute-start.3 = (f32[14,256,256]{1,2,0:T(8,128)}, f32[14,256,256]{1,2,0:T(8,128)}, u32[]{:S(2)}, u32[]{:S(2)}) collective-permute-start(f32[14,256,256]{1,2,0:T(8,128)} %convolution_bitcast_fusion.2), channel_id=1, source_target_pairs={{8,0},{9,1},{10,2},{11,3},{12,4},{13,5},{14,6},{15,7},{16,8},{17,9... | collective-permute-start | bytes 11010056 | tf_op jit(solution)/shard_map/ppermute | solution.py:13
  103.0 2.4 copy-start.2
  143.0 2.0 copy-start.1
  145.0 2.0 copy-start.3
  149.1 153.3 %collective-permute-start.2 = (bf16[14,256,256]{1,2,0:T(8,128)(2,1)}, bf16[14,256,256]{1,2,0:T(8,128)(2,1)}, u32[]{:S(2)}, u32[]{:S(2)}) collective-permute-start(bf16[14,256,256]{1,2,0:T(8,128)(2,1)} %fusion.17), channel_id=1, source_target_pairs={{0,8},{8,16},{16,24},{24,32},{32,40},{40,48},{48,56},{56,64},{64,7... | collective-permute-start | bytes 5505032 | tf_op jit(solution)/shard_map/ppermute | solution.py:13
  298.5 3.9 %copy-start.4 = (bf16[1,1,14,256,256]{3,4,2,1,0:T(8,128)(2,1)S(1)}, bf16[1,1,14,256,256]{3,4,2,1,0:T(8,128)(2,1)}, u32[]{:S(2)}) copy-start(bf16[1,1,14,256,256]{3,4,2,1,0:T(8,128)(2,1)} %copy.55) | copy-start | bytes 5505028
where the time goes:
time: 311 us; the launch traced here: 309 us
  waiting for transfers between devices  135 us (43%)
  local copies, waits for them, and re-layouts  87 us (28%)
  matrix products  46.8 us (15%)
  starting transfers between devices  19.6 us (6%)
  other arithmetic  15.2 us (5%)
  between operations  5.6 us (2%)
    ppermute x6, waiting for transfers between devices, from_behind(): lax.ppermute(value, axis, [(source, source + steps) for source in range(i...  135 us
    unnamed x36, local copies, waits for them, and re-layouts  25.4 us
    ppermute x6, starting transfers between devices, from_behind(): lax.ppermute(value, axis, [(source, source + steps) for source in range(i...  19.6 us
    another operation x3, local copies, waits for them, and re-layouts, left_group(): jnp.stack(products).reshape(group_size * mpo_width, slot_size * slot_size)  12.3 us
    another operation x3, local copies, waits for them, and re-layouts, right_group(): jnp.stack(products).reshape(group_size * mpo_width, slot_size * slot_size)  12.3 us
    dot_general x4, matrix products, left_group(): jnp.dot(flattened, operand, preferred_element_type=jnp.float32)  10.3 us
    broadcast_in_dim x2, other arithmetic, body(): return (left_out[None, None], right_out[None, None])  10.2 us
    dot_general x3, matrix products, left_group(): jnp.dot(left_mixer(weights, members), stacked, preferred_element_type=jnp...  9.27 us
  transfers between devices with their start and end apart: 6, of which 2 were waited for; matrix products, arithmetic and copies ran while one was open for 44% of the time, Pallas kernels for 0%

commit v1 on v0

v1 whole, which is shorter than its diff:
```python
import jax
import jax.numpy as jnp
from jax import lax
from jax.experimental import pallas as pl
from jax.experimental.pallas import tpu as pltpu
from jax.sharding import PartitionSpec as P

MESH = pl.DeviceIdType.MESH
BF = jnp.bfloat16
F32 = jnp.float32
OFFSETS = (0, 1, 1, 2)
STEP_ROWS = 32
UNIT_ROWS = 64
TILE = 16


def transposed_dot(a, b):
    return lax.dot_general(a, b, (((1,), (1,)), ((), ())), preferred_element_type=F32)


def kernel(
    chains, sectors,
    lenv, renv, lstate, rstate, mixers, couple, sizes,
    lout, rout,
    env, own, site, turned, mix0, mix3, mix12, inner, mixed, total, result,
    load_sem, x_send, x_recv, y_send, y_recv, d_send, d_recv, s_send, s_recv, out_sem,
):
    width, slot = lenv.shape[0], lenv.shape[1]
    steps, quarters = slot // STEP_ROWS, slot // UNIT_ROWS
    i = lax.axis_index("chain")
    k = lax.axis_index("sector")
    core = lax.rem(k, 2)

    def at(chain_step, sector_step):
        return (
            lax.rem(i + chain_step + chains, chains),
            lax.rem(k + sector_step + sectors, sectors),
        )

    partner = (i, k + 1 - 2 * core)
    ahead, behind = at(1, 0), at(-1, 0)
    barrier = pltpu.get_barrier_semaphore()
    greeted = (
        ahead, behind, at(0, 2), at(0, -2), partner,
        at(-1, -1), at(-1, -2), at(1, 1), at(1, 2),
    )
    for device in greeted:
        pl.semaphore_signal(barrier, inc=1, device_id=device, device_id_type=MESH)

    loads = [
        pltpu.make_async_copy(source, own.at[side], load_sem.at[side])
        for side, source in enumerate((lstate, rstate))
    ]
    for load in loads:
        load.start()
    pl.semaphore_wait(barrier, len(greeted))

    def rows(step):
        return pl.ds(pl.multiple_of(step * STEP_ROWS, STEP_ROWS), STEP_ROWS)

    def x_copy(side, step):
        return pltpu.make_async_remote_copy(
            (lenv, renv)[side].at[:, rows(step), :],
            env.at[side, 0, :, rows(step), :],
            x_send.at[side, step], x_recv.at[side, step],
            device_id=(ahead, behind)[side], device_id_type=MESH,
        )

    def y_copy(side, step):
        return pltpu.make_async_remote_copy(
            env.at[side, 0, :, rows(step), :],
            env.at[side, 2, :, rows(step), :],
            y_send.at[side, step], y_recv.at[side, step],
            device_id=(at(0, 2), at(0, -2))[side], device_id_type=MESH,
        )

    def d_copy(side, step):
        held = (2 * core, 2 * (1 - core))[side]
        return pltpu.make_async_remote_copy(
            env.at[side, held, :, rows(step), :],
            env.at[side, 1, :, rows(step), :],
            d_send.at[side, step], d_recv.at[side, step],
            device_id=partner, device_id_type=MESH,
        )

    def s_copy(n):
        side, first, count, device = (
            (0, 0, 4, ahead), (1, 0, 1, behind), (1, 1, 2, at(-1, -1)), (1, 3, 1, at(-1, -2)),
        )[n]
        return pltpu.make_async_remote_copy(
            own.at[side, pl.ds(first, count)],
            site.at[side, pl.ds(first, count)],
            s_send.at[n], s_recv.at[n],
            device_id=device, device_id_type=MESH,
        )

    for side in range(2):
        x_copy(side, 0).start()

    for load in loads:
        load.wait()
    row_ids = lax.broadcasted_iota(jnp.int32, (slot, slot), 0)
    col_ids = lax.broadcasted_iota(jnp.int32, (slot, slot), 1)
    for s in range(4):
        source = k - OFFSETS[s]
        live = jnp.where(source >= 0, sizes[jnp.maximum(source, 0)], 0)
        live = jnp.where(couple[s] > 0, live, 0)
        keep = (row_ids < live) & (col_ids < sizes[k])
        own[0, s] = jnp.where(keep, own[0, s].astype(F32), 0.0).astype(BF)
        own[1, s] = jnp.where(keep, own[1, s].astype(F32), 0.0).T.astype(BF)
    for n in range(4):
        s_copy(n).start()
    for side in range(2):
        x_copy(side, 1).start()

    def picker(count, first):
        shape = (count * TILE, mixers.shape[2])
        r = lax.broadcasted_iota(jnp.int32, shape, 0)
        c = lax.broadcasted_iota(jnp.int32, shape, 1)
        return jnp.where(r // TILE + first == c, 1.0, 0.0).astype(BF)

    def spread(side, count, first):
        pick = picker(count, first)
        part = jnp.dot(pick, mixers[side], preferred_element_type=F32).astype(BF)
        full = transposed_dot(part, pick)
        r = lax.broadcasted_iota(jnp.int32, full.shape, 0)
        c = lax.broadcasted_iota(jnp.int32, full.shape, 1)
        return jnp.where(lax.rem(r, TILE) == lax.rem(c, TILE), full, 0.0).astype(BF)

    for side in range(2):
        mix0[side] = spread(side, width, 0)
        mix3[side] = spread(side, width, 3 * width)
        mix12[side] = spread(side, 2 * width, width)

    def clear(v, carry):
        for side in range(2):
            total[side, v] = jnp.zeros((slot, slot), F32)
        return carry

    lax.fori_loop(0, width, clear, 0)

    def turn():
        for n in range(4):
            s_copy(n).wait_recv()
        for side in range(2):
            for q in range(quarters):
                part = site[side, :, q * UNIT_ROWS : (q + 1) * UNIT_ROWS, :]
                turned[side, q] = part.reshape(4 * UNIT_ROWS, slot).astype(F32).T.astype(BF)

    def unit(side, q):
        span = pl.ds(pl.multiple_of(q * UNIT_ROWS, UNIT_ROWS), UNIT_ROWS)

        def first(s, carry):
            held = env[side, (s + 1) // 2, :, span, :].reshape(width * UNIT_ROWS, slot)
            product = jnp.dot(held, site[side, s], preferred_element_type=F32)
            inner[s] = product.astype(BF).reshape(width, UNIT_ROWS, slot)
            return carry

        lax.fori_loop(0, 4, first, 0)

        def mix(a, carry):
            part = pl.ds(pl.multiple_of(a * TILE, TILE), TILE)
            for s, weights in ((0, mix0), (3, mix3)):
                held = inner[s, :, part, :].reshape(width * TILE, slot)
                product = jnp.dot(weights[side], held, preferred_element_type=F32)
                mixed[:, s, part, :] = product.astype(BF).reshape(width, TILE, slot)
            held = inner[1:3, :, part, :].reshape(2 * width * TILE, slot)
            product = jnp.dot(mix12[side], held, preferred_element_type=F32)
            product = product.astype(BF).reshape(2, width, TILE, slot)
            mixed[:, 1, part, :] = product[0]
            mixed[:, 2, part, :] = product[1]
            return carry

        lax.fori_loop(0, UNIT_ROWS // TILE, mix, 0)

        def last(v, carry):
            held = mixed[v].reshape(4 * UNIT_ROWS, slot)
            value = total[side, v] + jnp.dot(turned[side, q], held, preferred_element_type=F32)
            total[side, v] = value
            result[side, v] = value.astype(BF)
            return carry

        lax.fori_loop(0, width, last, 0)

    per_unit = UNIT_ROWS // STEP_ROWS

    def step(c, carry):
        @pl.when(c < steps)
        def _():
            for side in range(2):
                x_copy(side, c).wait_recv()
                y_copy(side, c).start()
                x_copy(side, c).wait_send()

        @pl.when(c + 2 < steps)
        def _():
            for side in range(2):
                x_copy(side, c + 2).start()

        @pl.when((c >= 1) & (c <= steps))
        def _():
            for side in range(2):
                y_copy(side, c - 1).wait_recv()
                d_copy(side, c - 1).start()

        @pl.when(c == per_unit)
        def _():
            turn()

        @pl.when(c >= per_unit + 1)
        def _():
            u = c - per_unit - 1
            side, q = lax.rem(u, 2), u // 2
            for part in range(per_unit):
                @pl.when(side == 0)
                def _():
                    d_copy(0, q * per_unit + part).wait_recv()

                @pl.when(side == 1)
                def _():
                    d_copy(1, q * per_unit + part).wait_recv()
            unit(side, q)

        return carry

    lax.fori_loop(0, 2 * quarters + per_unit + 1, step, 0)

    for side, (edge, source, target) in enumerate(((0, lenv, lout), (chains - 1, renv, rout))):
        @pl.when(i == edge)
        def _():
            pltpu.make_async_copy(source, target, out_sem.at[side]).start()

        @pl.when(i != edge)
        def _():
            pltpu.make_async_copy(result.at[side], target, out_sem.at[side]).start()

    for n in range(4):
        s_copy(n).wait_send()

    def settle(c, carry):
        for side in range(2):
            y_copy(side, c).wait_send()
            d_copy(side, c).wait_send()
        return carry

    lax.fori_loop(0, steps, settle, 0)
    for side, target in enumerate((lout, rout)):
        pltpu.make_async_copy(result.at[side], target, out_sem.at[side]).wait()


def body(chains, sectors, left_env, right_env, left_state, right_state, mpo, couple, sizes):
    width, slot = left_env.shape[2], left_env.shape[3]
    steps, quarters = slot // STEP_ROWS, slot // UNIT_ROWS
    mixers = jnp.stack(
        [
            jnp.transpose(mpo, (1, 3, 2, 0)).reshape(4 * width, 4 * width),
            jnp.transpose(mpo, (1, 0, 2, 3)).reshape(4 * width, 4 * width),
        ]
    )
    anywhere = pl.BlockSpec(memory_space=pl.ANY)
    scalars = pl.BlockSpec(memory_space=pltpu.SMEM)
    dma = pltpu.SemaphoreType.DMA

    def run(*refs):
        kernel(chains, sectors, *refs)

    flops = 2 * 2 * width * slot * slot * (8 * slot + 6 * width)
    left_out, right_out = pl.pallas_call(
        run,
        out_shape=[jax.ShapeDtypeStruct((width, slot, slot), BF)] * 2,
        in_specs=[anywhere] * 4 + [pl.BlockSpec(memory_space=pltpu.VMEM), scalars, scalars],
        out_specs=[anywhere] * 2,
        scratch_shapes=[
            pltpu.VMEM((2, 3, width, slot, slot), BF),
            pltpu.VMEM((2, 4, slot, slot), BF),
            pltpu.VMEM((2, 4, slot, slot), BF),
            pltpu.VMEM((2, quarters, slot, 4 * UNIT_ROWS), BF),
            pltpu.VMEM((2, width * TILE, width * TILE), BF),
            pltpu.VMEM((2, width * TILE, width * TILE), BF),
            pltpu.VMEM((2, 2 * width * TILE, 2 * width * TILE), BF),
            pltpu.VMEM((4, width, UNIT_ROWS, slot), BF),
            pltpu.VMEM((width, 4, UNIT_ROWS, slot), BF),
            pltpu.VMEM((2, width, slot, slot), F32),
            pltpu.VMEM((2, width, slot, slot), BF),
            dma((2,)),
            dma((2, steps)), dma((2, steps)),
            dma((2, steps)), dma((2, steps)),
            dma((2, steps)), dma((2, steps)),
            dma((4,)), dma((4,)),
            dma((2,)),
        ],
        compiler_params=pltpu.CompilerParams(
            collective_id=0, has_side_effects=True, vmem_limit_bytes=60 << 20
        ),
        cost_estimate=pl.CostEstimate(flops=flops, bytes_accessed=10 << 20, transcendentals=0),
    )(
        left_env[0, 0], right_env[0, 0], left_state[0, 0], right_state[0, 0],
        mixers, couple[0, :, 0], sizes,
    )
    return left_out[None, None], right_out[None, None]


def solution(mesh):
    blocks = P("chain", "sector", None, None, None)
    chains, sectors = mesh.shape["chain"], mesh.shape["sector"]

    def run(*args):
        return body(chains, sectors, *args)

    return jax.shard_map(
        run,
        mesh=mesh,
        in_specs=(blocks, blocks, blocks, blocks, P(), P("chain", None, "sector"), P()),
        out_specs=(blocks, blocks),
        check_vma=False,
    )
```

time: 311 us -> 157 us (0.50)
  the two profiles are of different devices: /device:TPU:39 before, /device:TPU:8 now
where the time goes in v1:
time: 157 us
  Pallas kernels  149 us (95%)
  local copies, waits for them, and re-layouts  6.31 us (4%)
    pallas_call x1, Pallas kernels, body(): pl.pallas_call(run, out_shape=[jax.ShapeDtypeStruct((width, slot, slot),...  149 us
    unnamed x4, local copies, waits for them, and re-layouts  4.23 us

profile of v1, /device:TPU:8, one launch (start us, length us, event | category | flops | bytes accessed | tf_op | source)
XLA Modules:
  0.0 156.5 jit_solution(3895203704162838779)
XLA Ops:
  0.6 1.0 copy.9
  1.7 0.1 stack_reshape.6
  1.8 0.8 copy.10
  2.6 0.1 stack_reshape.7
  2.7 0.6 pad_maximum_fusion.refs_4_
  3.3 148.9 %shard_map.86 = (bf16[14,256,256]{2,1,0:T(8,128)(2,1)}, bf16[14,256,256]{2,1,0:T(8,128)(2,1)}) custom-call(bf16[14,256,256]{2,1,0:T(8,128)(2,1)} %bitcast.13, bf16[14,256,256]{2,1,0:T(8,128)(2,1)} %bitcast.14, bf16[4,256,256]{2,1,0:T(8,128)(2,1)} %bitcast.15, bf16[4,256,256]{2,1,0:T(8,128)(2,1)} %bitcast.16, bf16[2,56,56]{2,1,0:T(8,128)(2,1)} %pad_maximum_fusion.refs_4_, ...), custom_call_target="tpu_custom_call" | custom-call | flops 7824474112 | bytes 10485760 | tf_op jit(solution)/shard_map/pallas_call | solution.py:268
  152.3 0.0 copy-start
  152.3 3.0 %copy.13 = bf16[1,1,14,256,256]{4,3,2,1,0:T(8,128)(2,1)} copy(bf16[1,1,14,256,256]{4,3,2,1,0:T(8,128)(2,1)} %bitcast.10) | data formatting | bytes 3670016
  155.3 0.0 copy-done
  155.3 1.2 copy.14
Async XLA Ops:
  152.3 3.0 %copy-start = (bf16[14,256,256]{2,1,0:T(8,128)(2,1)S(1)}, bf16[14,256,256]{2,1,0:T(8,128)(2,1)}, u32[]{:S(2)}) copy-start(bf16[14,256,256]{2,1,0:T(8,128)(2,1)} %get-tuple-element.5) | copy-start | bytes 5505028

commit v2 on v1

--- a/solution.py
+++ b/solution.py
@@ -10,7 +10,8 @@
 F32 = jnp.float32
 OFFSETS = (0, 1, 1, 2)
 STEP_ROWS = 32
-UNIT_ROWS = 64
+UNIT_ROWS = 32
+DEPTH = 2
 TILE = 16
 
 
@@ -20,10 +21,10 @@
 
 def kernel(
     chains, sectors,
-    lenv, renv, lstate, rstate, mixers, couple, sizes,
+    lenv, renv, lstate, rstate, mpo, couple, sizes,
     lout, rout,
-    env, own, site, turned, mix0, mix3, mix12, inner, mixed, total, result,
-    load_sem, x_send, x_recv, y_send, y_recv, d_send, d_recv, s_send, s_recv, out_sem,
+    env, own, site, turned, mix0, mix3, mix12, inner, mixed, total, result, kept,
+    load_sem, x_send, x_recv, y_send, y_recv, d_send, d_recv, s_send, s_recv, kept_sem, out_sem,
 ):
     width, slot = lenv.shape[0], lenv.shape[1]
     steps, quarters = slot // STEP_ROWS, slot // UNIT_ROWS
@@ -83,6 +84,14 @@
             device_id=partner, device_id_type=MESH,
         )
 
+    def d_wait(side, step):
+        pltpu.make_async_remote_copy(
+            env.at[side, 0, :, rows(step), :],
+            env.at[side, 1, :, rows(step), :],
+            d_send.at[side, step], d_recv.at[side, step],
+            device_id=partner, device_id_type=MESH,
+        ).wait_recv()
+
     def s_copy(n):
         side, first, count, device = (
             (0, 0, 4, ahead), (1, 0, 1, behind), (1, 1, 2, at(-1, -1)), (1, 3, 1, at(-1, -2)),
@@ -96,6 +105,16 @@
 
     for side in range(2):
         x_copy(side, 0).start()
+
+    edges = ((0, lenv, lout), (chains - 1, renv, rout))
+
+    def keep_copy(side):
+        return pltpu.make_async_copy(edges[side][1], kept.at[side], kept_sem.at[side])
+
+    for side in range(2):
+        @pl.when(i == edges[side][0])
+        def _():
+            keep_copy(side).start()
 
     for load in loads:
         load.wait()
@@ -110,27 +129,43 @@
         own[1, s] = jnp.where(keep, own[1, s].astype(F32), 0.0).T.astype(BF)
     for n in range(4):
         s_copy(n).start()
-    for side in range(2):
-        x_copy(side, 1).start()
-
-    def picker(count, first):
-        shape = (count * TILE, mixers.shape[2])
+    for n in range(1, DEPTH):
+        for side in range(2):
+            x_copy(side, n).start()
+
+    def picker(count, member):
+        shape = (count * width * TILE, width)
         r = lax.broadcasted_iota(jnp.int32, shape, 0)
         c = lax.broadcasted_iota(jnp.int32, shape, 1)
-        return jnp.where(r // TILE + first == c, 1.0, 0.0).astype(BF)
-
-    def spread(side, count, first):
-        pick = picker(count, first)
-        part = jnp.dot(pick, mixers[side], preferred_element_type=F32).astype(BF)
-        full = transposed_dot(part, pick)
+        return jnp.where(r // TILE == c + member * width, 1.0, 0.0).astype(BF)
+
+    def entries(s, t):
+        r = lax.broadcasted_iota(jnp.int32, (width, width), 0)
+        found = jnp.zeros((width, width), F32)
+        for w in range(width):
+            line = mpo[w, s].astype(F32)[t : t + 1, :]
+            found = jnp.where(r == w, jnp.broadcast_to(line, (width, width)), found)
+        return found.astype(BF)
+
+    def spread(side, members):
+        count = len(members)
+        picks = [picker(count, n) for n in range(count)]
+        full = jnp.zeros((count * width * TILE, count * width * TILE), F32)
+        for n in range(count):
+            part = jnp.zeros((count * width * TILE, width), F32)
+            for m in range(count):
+                pair = (members[n], members[m]) if side == 0 else (members[m], members[n])
+                part += jnp.dot(picks[m], entries(*pair), preferred_element_type=F32)
+            part = part.astype(BF)
+            full += transposed_dot(picks[n], part) if side == 0 else transposed_dot(part, picks[n])
         r = lax.broadcasted_iota(jnp.int32, full.shape, 0)
         c = lax.broadcasted_iota(jnp.int32, full.shape, 1)
         return jnp.where(lax.rem(r, TILE) == lax.rem(c, TILE), full, 0.0).astype(BF)
 
     for side in range(2):
-        mix0[side] = spread(side, width, 0)
-        mix3[side] = spread(side, width, 3 * width)
-        mix12[side] = spread(side, 2 * width, width)
+        mix0[side] = spread(side, (0,))
+        mix3[side] = spread(side, (3,))
+        mix12[side] = spread(side, (1, 2))
 
     def clear(v, carry):
         for side in range(2):
@@ -156,7 +191,7 @@
             inner[s] = product.astype(BF).reshape(width, UNIT_ROWS, slot)
             return carry
 
-        lax.fori_loop(0, 4, first, 0)
+        lax.fori_loop(0, 4, first, 0, unroll=True)
 
         def mix(a, carry):
             part = pl.ds(pl.multiple_of(a * TILE, TILE), TILE)
@@ -171,7 +206,7 @@
             mixed[:, 2, part, :] = product[1]
             return carry
 
-        lax.fori_loop(0, UNIT_ROWS // TILE, mix, 0)
+        lax.fori_loop(0, UNIT_ROWS // TILE, mix, 0, unroll=True)
 
         def last(v, carry):
             held = mixed[v].reshape(4 * UNIT_ROWS, slot)
@@ -180,7 +215,7 @@
             result[side, v] = value.astype(BF)
             return carry
 
-        lax.fori_loop(0, width, last, 0)
+        lax.fori_loop(0, width, last, 0, unroll=True)
 
     per_unit = UNIT_ROWS // STEP_ROWS
 
@@ -192,10 +227,10 @@
                 y_copy(side, c).start()
                 x_copy(side, c).wait_send()
 
-        @pl.when(c + 2 < steps)
+        @pl.when(c + DEPTH < steps)
         def _():
             for side in range(2):
-                x_copy(side, c + 2).start()
+                x_copy(side, c + DEPTH).start()
 
         @pl.when((c >= 1) & (c <= steps))
         def _():
@@ -207,28 +242,27 @@
         def _():
             turn()
 
-        @pl.when(c >= per_unit + 1)
-        def _():
-            u = c - per_unit - 1
-            side, q = lax.rem(u, 2), u // 2
-            for part in range(per_unit):
-                @pl.when(side == 0)
-                def _():
-                    d_copy(0, q * per_unit + part).wait_recv()
-
-                @pl.when(side == 1)
-                def _():
-                    d_copy(1, q * per_unit + part).wait_recv()
-            unit(side, q)
+        @pl.when((c > per_unit) & (lax.rem(c, per_unit) == 1 % per_unit))
+        def _():
+            q = (c - 2) // per_unit
+
+            def one(side, carry):
+                for part in range(per_unit):
+                    d_wait(side, q * per_unit + part)
+                unit(side, q)
+                return carry
+
+            lax.fori_loop(0, 2, one, 0)
 
         return carry
 
-    lax.fori_loop(0, 2 * quarters + per_unit + 1, step, 0)
-
-    for side, (edge, source, target) in enumerate(((0, lenv, lout), (chains - 1, renv, rout))):
+    lax.fori_loop(0, steps + 2, step, 0)
+
+    for side, (edge, source, target) in enumerate(edges):
         @pl.when(i == edge)
         def _():
-            pltpu.make_async_copy(source, target, out_sem.at[side]).start()
+            keep_copy(side).wait()
+            pltpu.make_async_copy(kept.at[side], target, out_sem.at[side]).start()
 
         @pl.when(i != edge)
         def _():
@@ -251,12 +285,6 @@
 def body(chains, sectors, left_env, right_env, left_state, right_state, mpo, couple, sizes):
     width, slot = left_env.shape[2], left_env.shape[3]
     steps, quarters = slot // STEP_ROWS, slot // UNIT_ROWS
-    mixers = jnp.stack(
-        [
-            jnp.transpose(mpo, (1, 3, 2, 0)).reshape(4 * width, 4 * width),
-            jnp.transpose(mpo, (1, 0, 2, 3)).reshape(4 * width, 4 * width),
-        ]
-    )
     anywhere = pl.BlockSpec(memory_space=pl.ANY)
     scalars = pl.BlockSpec(memory_space=pltpu.SMEM)
     dma = pltpu.SemaphoreType.DMA
@@ -282,12 +310,13 @@
             pltpu.VMEM((width, 4, UNIT_ROWS, slot), BF),
             pltpu.VMEM((2, width, slot, slot), F32),
             pltpu.VMEM((2, width, slot, slot), BF),
+            pltpu.VMEM((2, width, slot, slot), BF),
             dma((2,)),
             dma((2, steps)), dma((2, steps)),
             dma((2, steps)), dma((2, steps)),
             dma((2, steps)), dma((2, steps)),
             dma((4,)), dma((4,)),
-            dma((2,)),
+            dma((2,)), dma((2,)),
         ],
         compiler_params=pltpu.CompilerParams(
             collective_id=0, has_side_effects=True, vmem_limit_bytes=60 << 20
@@ -295,7 +324,7 @@
         cost_estimate=pl.CostEstimate(flops=flops, bytes_accessed=10 << 20, transcendentals=0),
     )(
         left_env[0, 0], right_env[0, 0], left_state[0, 0], right_state[0, 0],
-        mixers, couple[0, :, 0], sizes,
+        mpo, couple[0, :, 0], sizes,
     )
     return left_out[None, None], right_out[None, None]
 

time: 157 us -> 84.4 us (0.54)
  Pallas kernels: 149 us -> 79.4 us
  local copies, waits for them, and re-layouts: 6.31 us -> 4.23 us
    pallas_call x1, Pallas kernels: 149 us -> 79.4 us  [body(): pl.pallas_call(run, out_shape=[jax.ShapeDtypeStruct((width, slot, slot),...]
    transpose x2 -> x0, local copies, waits for them, and re-layouts: 1.88 us -> none  [the longest x1 1.04 us: body(): jnp.transpose(mpo, (1, 3, 2, 0)).reshape(4 * width, 4 * width)]
where the time goes in v2:
time: 84.4 us; the launch traced here: 84.3 us
  Pallas kernels  79.4 us (94%)
  local copies, waits for them, and re-layouts  4.23 us (5%)
    pallas_call x1, Pallas kernels, body(): pl.pallas_call(run, out_shape=[jax.ShapeDtypeStruct((width, slot, slot),...  79.4 us
    unnamed x4, local copies, waits for them, and re-layouts  4.23 us

profile of v2, /device:TPU:8, one launch (start us, length us, event | category | flops | bytes accessed | tf_op | source)
XLA Modules:
  0.0 84.3 jit_solution(11650842147309405792)
XLA Ops:
  0.6 79.4 %shard_map.86 = (bf16[14,256,256]{2,1,0:T(8,128)(2,1)}, bf16[14,256,256]{2,1,0:T(8,128)(2,1)}) custom-call(bf16[14,256,256]{2,1,0:T(8,128)(2,1)} %bitcast.9, bf16[14,256,256]{2,1,0:T(8,128)(2,1)} %bitcast.10, bf16[4,256,256]{2,1,0:T(8,128)(2,1)} %bitcast.11, bf16[4,256,256]{2,1,0:T(8,128)(2,1)} %bitcast.12, bf16[14,4,4,14]{3,2,1,0:T(4,128)(2,1)} %refs_4_.1, ...), custom_call_target="tpu_custom_call" | custom-call | flops 7824474112 | bytes 10485760 | tf_op jit(solution)/shard_map/pallas_call | solution.py:296
  80.0 0.0 copy-start
  80.0 3.0 %copy.11 = bf16[1,1,14,256,256]{4,3,2,1,0:T(8,128)(2,1)} copy(bf16[1,1,14,256,256]{4,3,2,1,0:T(8,128)(2,1)} %bitcast.8) | data formatting | bytes 3670016
  83.0 0.0 copy-done
  83.0 1.2 %copy.12 = bf16[1,1,14,256,256]{4,3,2,1,0:T(8,128)(2,1)} copy(bf16[1,1,14,256,256]{4,3,2,1,0:T(8,128)(2,1)S(1)} %bitcast.7) | data formatting | bytes 3670016
Async XLA Ops:
  80.0 3.0 %copy-start = (bf16[14,256,256]{2,1,0:T(8,128)(2,1)S(1)}, bf16[14,256,256]{2,1,0:T(8,128)(2,1)}, u32[]{:S(2)}) copy-start(bf16[14,256,256]{2,1,0:T(8,128)(2,1)} %get-tuple-element.5) | copy-start | bytes 5505028

commit v3 on v2

--- a/solution.py
+++ b/solution.py
@@ -10,8 +10,8 @@
 F32 = jnp.float32
 OFFSETS = (0, 1, 1, 2)
 STEP_ROWS = 32
-UNIT_ROWS = 32
-DEPTH = 2
+UNIT_ROWS = STEP_ROWS
+STATES = ((0,), (1, 2, 3))
 TILE = 16
 
 
@@ -22,12 +22,12 @@
 def kernel(
     chains, sectors,
     lenv, renv, lstate, rstate, mpo, couple, sizes,
-    lout, rout,
-    env, own, site, turned, mix0, mix3, mix12, inner, mixed, total, result, kept,
-    load_sem, x_send, x_recv, y_send, y_recv, d_send, d_recv, s_send, s_recv, kept_sem, out_sem,
+    result,
+    env, own, site, turned, mix0, mix3, mix12, inner, mixed, total,
+    load_sem, x_send, x_recv, y_send, y_recv, d_send, d_recv, s_send, s_recv, edge_sem,
 ):
     width, slot = lenv.shape[0], lenv.shape[1]
-    steps, quarters = slot // STEP_ROWS, slot // UNIT_ROWS
+    steps, units = slot // STEP_ROWS, slot // UNIT_ROWS
     i = lax.axis_index("chain")
     k = lax.axis_index("sector")
     core = lax.rem(k, 2)
@@ -41,12 +41,23 @@
     partner = (i, k + 1 - 2 * core)
     ahead, behind = at(1, 0), at(-1, 0)
     barrier = pltpu.get_barrier_semaphore()
-    greeted = (
-        ahead, behind, at(0, 2), at(0, -2), partner,
-        at(-1, -1), at(-1, -2), at(1, 1), at(1, 2),
-    )
-    for device in greeted:
-        pl.semaphore_signal(barrier, inc=1, device_id=device, device_id_type=MESH)
+    gets = (i > 0, i < chains - 1)
+    gives = (gets[1], gets[0])
+
+    def greet(*devices):
+        for device in devices:
+            pl.semaphore_signal(barrier, inc=1, device_id=device, device_id_type=MESH)
+
+    greet(at(0, 2), at(0, -2), partner)
+
+    @pl.when(gives[0])
+    def _():
+        greet(ahead, at(1, 1), at(1, 2))
+
+    @pl.when(gives[1])
+    def _():
+        greet(behind, at(-1, -1), at(-1, -2))
+
 
     loads = [
         pltpu.make_async_copy(source, own.at[side], load_sem.at[side])
@@ -54,7 +65,8 @@
     ]
     for load in loads:
         load.start()
-    pl.semaphore_wait(barrier, len(greeted))
+    ends = jnp.where(i == 0, 1, 0) + jnp.where(i == chains - 1, 1, 0)
+    pl.semaphore_wait(barrier, 9 - 3 * ends)
 
     def rows(step):
         return pl.ds(pl.multiple_of(step * STEP_ROWS, STEP_ROWS), STEP_ROWS)
@@ -103,18 +115,19 @@
             device_id=device, device_id_type=MESH,
         )
 
+    edges = ((0, lenv), (chains - 1, renv))
+
+    def edge_copy(side):
+        return pltpu.make_async_copy(edges[side][1], result.at[side], edge_sem.at[side])
+
     for side in range(2):
-        x_copy(side, 0).start()
-
-    edges = ((0, lenv, lout), (chains - 1, renv, rout))
-
-    def keep_copy(side):
-        return pltpu.make_async_copy(edges[side][1], kept.at[side], kept_sem.at[side])
-
-    for side in range(2):
+        @pl.when(gives[side])
+        def _():
+            x_copy(side, 0).start()
+
         @pl.when(i == edges[side][0])
         def _():
-            keep_copy(side).start()
+            edge_copy(side).start()
 
     for load in loads:
         load.wait()
@@ -127,11 +140,20 @@
         keep = (row_ids < live) & (col_ids < sizes[k])
         own[0, s] = jnp.where(keep, own[0, s].astype(F32), 0.0).astype(BF)
         own[1, s] = jnp.where(keep, own[1, s].astype(F32), 0.0).T.astype(BF)
-    for n in range(4):
-        s_copy(n).start()
-    for n in range(1, DEPTH):
-        for side in range(2):
-            x_copy(side, n).start()
+    for side in range(2):
+        @pl.when(gives[side])
+        def _():
+            for n in STATES[side]:
+                s_copy(n).start()
+
+    def send(n, carry):
+        for side in range(2):
+            @pl.when(gives[side])
+            def _():
+                x_copy(side, n).start()
+        return carry
+
+    lax.fori_loop(1, steps, send, 0)
 
     def picker(count, member):
         shape = (count * width * TILE, width)
@@ -175,26 +197,23 @@
     lax.fori_loop(0, width, clear, 0)
 
     def turn():
-        for n in range(4):
-            s_copy(n).wait_recv()
-        for side in range(2):
-            for q in range(quarters):
-                part = site[side, :, q * UNIT_ROWS : (q + 1) * UNIT_ROWS, :]
-                turned[side, q] = part.reshape(4 * UNIT_ROWS, slot).astype(F32).T.astype(BF)
+        for side in range(2):
+            @pl.when(gets[side])
+            def _():
+                for n in STATES[side]:
+                    s_copy(n).wait_recv()
+                for q in range(units):
+                    part = site[side, :, q * UNIT_ROWS : (q + 1) * UNIT_ROWS, :]
+                    turned[side, q] = part.reshape(4 * UNIT_ROWS, slot).astype(F32).T.astype(BF)
 
     def unit(side, q):
         span = pl.ds(pl.multiple_of(q * UNIT_ROWS, UNIT_ROWS), UNIT_ROWS)
-
-        def first(s, carry):
+        for s in range(4):
             held = env[side, (s + 1) // 2, :, span, :].reshape(width * UNIT_ROWS, slot)
             product = jnp.dot(held, site[side, s], preferred_element_type=F32)
             inner[s] = product.astype(BF).reshape(width, UNIT_ROWS, slot)
-            return carry
-
-        lax.fori_loop(0, 4, first, 0, unroll=True)
-
-        def mix(a, carry):
-            part = pl.ds(pl.multiple_of(a * TILE, TILE), TILE)
+        for a in range(UNIT_ROWS // TILE):
+            part = pl.ds(a * TILE, TILE)
             for s, weights in ((0, mix0), (3, mix3)):
                 held = inner[s, :, part, :].reshape(width * TILE, slot)
                 product = jnp.dot(weights[side], held, preferred_element_type=F32)
@@ -204,52 +223,40 @@
             product = product.astype(BF).reshape(2, width, TILE, slot)
             mixed[:, 1, part, :] = product[0]
             mixed[:, 2, part, :] = product[1]
-            return carry
-
-        lax.fori_loop(0, UNIT_ROWS // TILE, mix, 0, unroll=True)
-
-        def last(v, carry):
+        for v in range(width):
             held = mixed[v].reshape(4 * UNIT_ROWS, slot)
             value = total[side, v] + jnp.dot(turned[side, q], held, preferred_element_type=F32)
             total[side, v] = value
             result[side, v] = value.astype(BF)
-            return carry
-
-        lax.fori_loop(0, width, last, 0, unroll=True)
-
-    per_unit = UNIT_ROWS // STEP_ROWS
+
+    def got(side):
+        return jnp.where(side == 0, i, chains - 1 - i) > 0
 
     def step(c, carry):
-        @pl.when(c < steps)
-        def _():
-            for side in range(2):
+        for side in range(2):
+            @pl.when((c < steps) & gets[side])
+            def _():
                 x_copy(side, c).wait_recv()
                 y_copy(side, c).start()
-                x_copy(side, c).wait_send()
-
-        @pl.when(c + DEPTH < steps)
-        def _():
-            for side in range(2):
-                x_copy(side, c + DEPTH).start()
-
-        @pl.when((c >= 1) & (c <= steps))
-        def _():
-            for side in range(2):
+
+        for side in range(2):
+            @pl.when((c >= 1) & (c <= steps) & gets[side])
+            def _():
                 y_copy(side, c - 1).wait_recv()
                 d_copy(side, c - 1).start()
 
-        @pl.when(c == per_unit)
+        @pl.when(c == 1)
         def _():
             turn()
 
-        @pl.when((c > per_unit) & (lax.rem(c, per_unit) == 1 % per_unit))
-        def _():
-            q = (c - 2) // per_unit
-
+        @pl.when(c >= 2)
+        def _():
             def one(side, carry):
-                for part in range(per_unit):
-                    d_wait(side, q * per_unit + part)
-                unit(side, q)
+                @pl.when(got(side))
+                def _():
+                    d_wait(side, c - 2)
+                    unit(side, c - 2)
+
                 return carry
 
             lax.fori_loop(0, 2, one, 0)
@@ -258,33 +265,33 @@
 
     lax.fori_loop(0, steps + 2, step, 0)
 
-    for side, (edge, source, target) in enumerate(edges):
-        @pl.when(i == edge)
-        def _():
-            keep_copy(side).wait()
-            pltpu.make_async_copy(kept.at[side], target, out_sem.at[side]).start()
-
-        @pl.when(i != edge)
-        def _():
-            pltpu.make_async_copy(result.at[side], target, out_sem.at[side]).start()
-
-    for n in range(4):
-        s_copy(n).wait_send()
-
     def settle(c, carry):
         for side in range(2):
-            y_copy(side, c).wait_send()
-            d_copy(side, c).wait_send()
+            @pl.when(gives[side])
+            def _():
+                x_copy(side, c).wait_send()
+
+            @pl.when(gets[side])
+            def _():
+                y_copy(side, c).wait_send()
+                d_copy(side, c).wait_send()
         return carry
 
     lax.fori_loop(0, steps, settle, 0)
-    for side, target in enumerate((lout, rout)):
-        pltpu.make_async_copy(result.at[side], target, out_sem.at[side]).wait()
+    for side in range(2):
+        @pl.when(gives[side])
+        def _():
+            for n in STATES[side]:
+                s_copy(n).wait_send()
+
+        @pl.when(i == edges[side][0])
+        def _():
+            edge_copy(side).wait()
 
 
 def body(chains, sectors, left_env, right_env, left_state, right_state, mpo, couple, sizes):
     width, slot = left_env.shape[2], left_env.shape[3]
-    steps, quarters = slot // STEP_ROWS, slot // UNIT_ROWS
+    steps, units = slot // STEP_ROWS, slot // UNIT_ROWS
     anywhere = pl.BlockSpec(memory_space=pl.ANY)
     scalars = pl.BlockSpec(memory_space=pltpu.SMEM)
     dma = pltpu.SemaphoreType.DMA
@@ -293,30 +300,28 @@
         kernel(chains, sectors, *refs)
 
     flops = 2 * 2 * width * slot * slot * (8 * slot + 6 * width)
-    left_out, right_out = pl.pallas_call(
+    out = pl.pallas_call(
         run,
-        out_shape=[jax.ShapeDtypeStruct((width, slot, slot), BF)] * 2,
+        out_shape=pltpu.VMEM((2, width, slot, slot), BF),
         in_specs=[anywhere] * 4 + [pl.BlockSpec(memory_space=pltpu.VMEM), scalars, scalars],
-        out_specs=[anywhere] * 2,
+        out_specs=pl.BlockSpec(memory_space=pltpu.VMEM),
         scratch_shapes=[
             pltpu.VMEM((2, 3, width, slot, slot), BF),
             pltpu.VMEM((2, 4, slot, slot), BF),
             pltpu.VMEM((2, 4, slot, slot), BF),
-            pltpu.VMEM((2, quarters, slot, 4 * UNIT_ROWS), BF),
+            pltpu.VMEM((2, units, slot, 4 * UNIT_ROWS), BF),
             pltpu.VMEM((2, width * TILE, width * TILE), BF),
             pltpu.VMEM((2, width * TILE, width * TILE), BF),
             pltpu.VMEM((2, 2 * width * TILE, 2 * width * TILE), BF),
             pltpu.VMEM((4, width, UNIT_ROWS, slot), BF),
             pltpu.VMEM((width, 4, UNIT_ROWS, slot), BF),
             pltpu.VMEM((2, width, slot, slot), F32),
-            pltpu.VMEM((2, width, slot, slot), BF),
-            pltpu.VMEM((2, width, slot, slot), BF),
             dma((2,)),
             dma((2, steps)), dma((2, steps)),
             dma((2, steps)), dma((2, steps)),
             dma((2, steps)), dma((2, steps)),
             dma((4,)), dma((4,)),
-            dma((2,)), dma((2,)),
+            dma((2,)),
         ],
         compiler_params=pltpu.CompilerParams(
             collective_id=0, has_side_effects=True, vmem_limit_bytes=60 << 20
@@ -326,7 +331,7 @@
         left_env[0, 0], right_env[0, 0], left_state[0, 0], right_state[0, 0],
         mpo, couple[0, :, 0], sizes,
     )
-    return left_out[None, None], right_out[None, None]
+    return out[0][None, None], out[1][None, None]
 
 
 def solution(mesh):

time: 84.4 us -> 76.4 us (0.905)
  the two profiles are of different devices: /device:TPU:8 before, /device:TPU:128 now
where the time goes in v3:
time: 76.4 us; the launch traced here: 76.3 us
  Pallas kernels  73.4 us (96%)
  local copies, waits for them, and re-layouts  2.22 us (3%)
    pallas_call x1, Pallas kernels, body(): pl.pallas_call(run, out_shape=pltpu.VMEM((2, width, slot, slot), BF), in_...  73.4 us
    another operation x1, local copies, waits for them, and re-layouts, body(): return (out[0][None, None], out[1][None, None])  2.22 us

profile of v3, /device:TPU:128, one launch (start us, length us, event | category | flops | bytes accessed | tf_op | source)
XLA Modules:
  0.0 76.3 jit_solution(9897970746632975417)
XLA Ops:
  0.6 73.4 %shard_map.86 = bf16[2,14,256,256]{3,2,1,0:T(8,128)(2,1)S(1)} custom-call(bf16[14,256,256]{2,1,0:T(8,128)(2,1)} %bitcast.9, bf16[14,256,256]{2,1,0:T(8,128)(2,1)} %bitcast.10, bf16[4,256,256]{2,1,0:T(8,128)(2,1)} %bitcast.11, bf16[4,256,256]{2,1,0:T(8,128)(2,1)} %bitcast.12, bf16[14,4,4,14]{3,2,1,0:T(4,128)(2,1)} %refs_4_.1, s32[4]{0:T(128)} %bitcast.13, ...), custom_call_target="tpu_custom_call" | custom-call | flops 7824474112 | bytes 10485760 | tf_op jit(solution)/shard_map/pallas_call | solution.py:303
  74.0 2.2 %slice_bitcast_fusion = (bf16[1,1,14,256,256]{4,3,2,1,0:T(8,128)(2,1)}, bf16[1,1,14,256,256]{4,3,2,1,0:T(8,128)(2,1)}) fusion(bf16[2,14,256,256]{3,2,1,0:T(8,128)(2,1)S(1)} %shard_map.86), kind=kLoop, calls=%fused_computation | loop fusion | bytes 7340032 | tf_op jit(solution)/shard_map/broadcast_in_dim;squeeze | solution.py:334

commit v4 on v3

--- a/solution.py
+++ b/solution.py
@@ -10,9 +10,12 @@
 F32 = jnp.float32
 OFFSETS = (0, 1, 1, 2)
 STEP_ROWS = 32
-UNIT_ROWS = STEP_ROWS
+UNIT_ROWS = 32
+LAG = 1
 STATES = ((0,), (1, 2, 3))
 TILE = 16
+PARTS = 2
+HALF = 8
 
 
 def transposed_dot(a, b):
@@ -155,11 +158,11 @@
 
     lax.fori_loop(1, steps, send, 0)
 
-    def picker(count, member):
-        shape = (count * width * TILE, width)
+    def picker(count, member, tile):
+        shape = (count * width * tile, width)
         r = lax.broadcasted_iota(jnp.int32, shape, 0)
         c = lax.broadcasted_iota(jnp.int32, shape, 1)
-        return jnp.where(r // TILE == c + member * width, 1.0, 0.0).astype(BF)
+        return jnp.where(r // tile == c + member * width, 1.0, 0.0).astype(BF)
 
     def entries(s, t):
         r = lax.broadcasted_iota(jnp.int32, (width, width), 0)
@@ -169,12 +172,12 @@
             found = jnp.where(r == w, jnp.broadcast_to(line, (width, width)), found)
         return found.astype(BF)
 
-    def spread(side, members):
+    def spread(side, members, tile):
         count = len(members)
-        picks = [picker(count, n) for n in range(count)]
-        full = jnp.zeros((count * width * TILE, count * width * TILE), F32)
+        picks = [picker(count, n, tile) for n in range(count)]
+        full = jnp.zeros((count * width * tile, count * width * tile), F32)
         for n in range(count):
-            part = jnp.zeros((count * width * TILE, width), F32)
+            part = jnp.zeros((count * width * tile, width), F32)
             for m in range(count):
                 pair = (members[n], members[m]) if side == 0 else (members[m], members[n])
                 part += jnp.dot(picks[m], entries(*pair), preferred_element_type=F32)
@@ -182,12 +185,12 @@
             full += transposed_dot(picks[n], part) if side == 0 else transposed_dot(part, picks[n])
         r = lax.broadcasted_iota(jnp.int32, full.shape, 0)
         c = lax.broadcasted_iota(jnp.int32, full.shape, 1)
-        return jnp.where(lax.rem(r, TILE) == lax.rem(c, TILE), full, 0.0).astype(BF)
+        return jnp.where(lax.rem(r, tile) == lax.rem(c, tile), full, 0.0).astype(BF)
 
     for side in range(2):
-        mix0[side] = spread(side, (0,))
-        mix3[side] = spread(side, (3,))
-        mix12[side] = spread(side, (1, 2))
+        mix0[side] = spread(side, (0,), TILE)
+        mix3[side] = spread(side, (3,), TILE)
+        mix12[side] = spread(side, (1, 2), HALF)
 
     def clear(v, carry):
         for side in range(2):
@@ -218,9 +221,13 @@
                 held = inner[s, :, part, :].reshape(width * TILE, slot)
                 product = jnp.dot(weights[side], held, preferred_element_type=F32)
                 mixed[:, s, part, :] = product.astype(BF).reshape(width, TILE, slot)
-            held = inner[1:3, :, part, :].reshape(2 * width * TILE, slot)
-            product = jnp.dot(mix12[side], held, preferred_element_type=F32)
-            product = product.astype(BF).reshape(2, width, TILE, slot)
+            held = inner[1:3, :, part, :].astype(F32)
+            halves = []
+            for h in range(2):
+                some = held[:, :, h * HALF : (h + 1) * HALF, :].reshape(2 * width * HALF, slot)
+                product = jnp.dot(mix12[side], some.astype(BF), preferred_element_type=F32)
+                halves.append(product.reshape(2, width, HALF, slot))
+            product = jnp.concatenate(halves, axis=2).astype(BF)
             mixed[:, 1, part, :] = product[0]
             mixed[:, 2, part, :] = product[1]
         for v in range(width):
@@ -232,6 +239,8 @@
     def got(side):
         return jnp.where(side == 0, i, chains - 1 - i) > 0
 
+    per_unit = UNIT_ROWS // STEP_ROWS
+
     def step(c, carry):
         for side in range(2):
             @pl.when((c < steps) & gets[side])
@@ -240,22 +249,25 @@
                 y_copy(side, c).start()
 
         for side in range(2):
-            @pl.when((c >= 1) & (c <= steps) & gets[side])
-            def _():
-                y_copy(side, c - 1).wait_recv()
-                d_copy(side, c - 1).start()
+            @pl.when((c >= LAG) & (c < steps + LAG) & gets[side])
+            def _():
+                y_copy(side, c - LAG).wait_recv()
+                d_copy(side, c - LAG).start()
 
         @pl.when(c == 1)
         def _():
             turn()
 
-        @pl.when(c >= 2)
-        def _():
+        @pl.when((c >= per_unit + LAG) & (lax.rem(c - LAG, per_unit) == 0))
+        def _():
+            q = (c - LAG) // per_unit - 1
+
             def one(side, carry):
                 @pl.when(got(side))
                 def _():
-                    d_wait(side, c - 2)
-                    unit(side, c - 2)
+                    for part in range(per_unit):
+                        d_wait(side, q * per_unit + part)
+                    unit(side, q)
 
                 return carry
 
@@ -263,7 +275,7 @@
 
         return carry
 
-    lax.fori_loop(0, steps + 2, step, 0)
+    lax.fori_loop(0, steps + LAG + 1, step, 0)
 
     def settle(c, carry):
         for side in range(2):
@@ -287,6 +299,21 @@
         @pl.when(i == edges[side][0])
         def _():
             edge_copy(side).wait()
+
+
+def write_out(result, lout, rout, sems):
+    size = lout.shape[0] // PARTS
+    copies = [
+        pltpu.make_async_copy(
+            result.at[side, pl.ds(part * size, size)], target.at[pl.ds(part * size, size)], sems.at[side, part]
+        )
+        for part in range(PARTS)
+        for side, target in enumerate((lout, rout))
+    ]
+    for copy in copies:
+        copy.start()
+    for copy in copies:
+        copy.wait()
 
 
 def body(chains, sectors, left_env, right_env, left_state, right_state, mpo, couple, sizes):
@@ -312,7 +339,7 @@
             pltpu.VMEM((2, units, slot, 4 * UNIT_ROWS), BF),
             pltpu.VMEM((2, width * TILE, width * TILE), BF),
             pltpu.VMEM((2, width * TILE, width * TILE), BF),
-            pltpu.VMEM((2, 2 * width * TILE, 2 * width * TILE), BF),
+            pltpu.VMEM((2, 2 * width * HALF, 2 * width * HALF), BF),
             pltpu.VMEM((4, width, UNIT_ROWS, slot), BF),
             pltpu.VMEM((width, 4, UNIT_ROWS, slot), BF),
             pltpu.VMEM((2, width, slot, slot), F32),
@@ -331,7 +358,15 @@
         left_env[0, 0], right_env[0, 0], left_state[0, 0], right_state[0, 0],
         mpo, couple[0, :, 0], sizes,
     )
-    return out[0][None, None], out[1][None, None]
+    left_out, right_out = pl.pallas_call(
+        write_out,
+        out_shape=[jax.ShapeDtypeStruct((width, slot, slot), BF)] * 2,
+        in_specs=[pl.BlockSpec(memory_space=pltpu.VMEM)],
+        out_specs=[anywhere] * 2,
+        scratch_shapes=[dma((2, PARTS))],
+        compiler_params=pltpu.CompilerParams(vmem_limit_bytes=16 << 20),
+    )(out)
+    return left_out[None, None], right_out[None, None]
 
 
 def solution(mesh):

time: 76.4 us -> 75.3 us (0.986)
  local copies, waits for them, and re-layouts: 2.22 us -> 0 us
  Pallas kernels: 73.4 us -> 74.5 us
    another operation x1 -> x0, local copies, waits for them, and re-layouts: 2.22 us -> none  [body(): return (out[0][None, None], out[1][None, None])]
    pallas_call x0 -> x1, Pallas kernels: none -> 1.87 us  [body(): pl.pallas_call(write_out, out_shape=[jax.ShapeDtypeStruct((width, slot, s...]
where the time goes in v4:
time: 75.3 us; the launch traced here: 75.2 us
  Pallas kernels  74.5 us (99%)
    pallas_call x1, Pallas kernels, body(): pl.pallas_call(run, out_shape=pltpu.VMEM((2, width, slot, slot), BF), in_...  72.6 us
    pallas_call x1, Pallas kernels, body(): pl.pallas_call(write_out, out_shape=[jax.ShapeDtypeStruct((width, slot, s...  1.87 us

profile of v4, /device:TPU:128, one launch (start us, length us, event | category | flops | bytes accessed | tf_op | source)
XLA Modules:
  0.0 75.2 jit_solution(1775344632852602324)
XLA Ops:
  0.6 72.6 %shard_map.86.result = bf16[2,14,256,256]{3,2,1,0:T(8,128)(2,1)S(1)} custom-call(bf16[14,256,256]{2,1,0:T(8,128)(2,1)} %bitcast.7, bf16[14,256,256]{2,1,0:T(8,128)(2,1)} %bitcast.8, bf16[4,256,256]{2,1,0:T(8,128)(2,1)} %bitcast.11, bf16[4,256,256]{2,1,0:T(8,128)(2,1)} %bitcast.12, bf16[14,4,4,14]{3,2,1,0:T(4,128)(2,1)} %refs_4_.1, s32[4]{0:T(128)} %bitcast.13, ...), custom_call_target="tpu_custom_call" | custom-call | flops 7824474112 | bytes 10485760 | tf_op jit(solution)/shard_map/pallas_call | solution.py:330
  73.3 1.9 %shard_map.87 = (bf16[14,256,256]{2,1,0:T(8,128)(2,1)}, bf16[14,256,256]{2,1,0:T(8,128)(2,1)}) custom-call(bf16[2,14,256,256]{3,2,1,0:T(8,128)(2,1)S(1)} %shard_map.86.result), custom_call_target="tpu_custom_call" | custom-call | tf_op jit(solution)/shard_map/pallas_call | solution.py:361

commit v5 on v4

--- a/solution.py
+++ b/solution.py
@@ -10,8 +10,7 @@
 F32 = jnp.float32
 OFFSETS = (0, 1, 1, 2)
 STEP_ROWS = 32
-UNIT_ROWS = 32
-LAG = 1
+UNIT_ROWS = STEP_ROWS
 STATES = ((0,), (1, 2, 3))
 TILE = 16
 PARTS = 2
@@ -239,8 +238,6 @@
     def got(side):
         return jnp.where(side == 0, i, chains - 1 - i) > 0
 
-    per_unit = UNIT_ROWS // STEP_ROWS
-
     def step(c, carry):
         for side in range(2):
             @pl.when((c < steps) & gets[side])
@@ -248,34 +245,31 @@
                 x_copy(side, c).wait_recv()
                 y_copy(side, c).start()
 
-        for side in range(2):
-            @pl.when((c >= LAG) & (c < steps + LAG) & gets[side])
-            def _():
-                y_copy(side, c - LAG).wait_recv()
-                d_copy(side, c - LAG).start()
-
         @pl.when(c == 1)
         def _():
             turn()
 
-        @pl.when((c >= per_unit + LAG) & (lax.rem(c - LAG, per_unit) == 0))
-        def _():
-            q = (c - LAG) // per_unit - 1
-
-            def one(side, carry):
-                @pl.when(got(side))
-                def _():
-                    for part in range(per_unit):
-                        d_wait(side, q * per_unit + part)
-                    unit(side, q)
-
-                return carry
-
-            lax.fori_loop(0, 2, one, 0)
+        def one(side, carry):
+            @pl.when(got(side) & (c >= 2))
+            def _():
+                d_wait(side, c - 2)
+                unit(side, c - 2)
+
+            @pl.when((c >= 1) & (c <= steps) & (side == 0))
+            def _():
+                for other in range(2):
+                    @pl.when(gets[other])
+                    def _():
+                        y_copy(other, c - 1).wait_recv()
+                        d_copy(other, c - 1).start()
+
+            return carry
+
+        lax.fori_loop(0, 2, one, 0)
 
         return carry
 
-    lax.fori_loop(0, steps + LAG + 1, step, 0)
+    lax.fori_loop(0, steps + 2, step, 0)
 
     def settle(c, carry):
         for side in range(2):

time: 75.3 us -> 73.9 us (0.981)
  Pallas kernels: 74.5 us -> 73.1 us
    pallas_call x1, Pallas kernels: 72.6 us -> 71.3 us  [body(): pl.pallas_call(run, out_shape=pltpu.VMEM((2, width, slot, slot), BF), in_...]
where the time goes in v5:
time: 73.9 us; the launch traced here: 73.8 us
  Pallas kernels  73.1 us (99%)
    pallas_call x1, Pallas kernels, body(): pl.pallas_call(run, out_shape=pltpu.VMEM((2, width, slot, slot), BF), in_...  71.3 us
    pallas_call x1, Pallas kernels, body(): pl.pallas_call(write_out, out_shape=[jax.ShapeDtypeStruct((width, slot, s...  1.87 us

profile of v5, /device:TPU:128, one launch (start us, length us, event | category | flops | bytes accessed | tf_op | source)
XLA Modules:
  0.0 73.8 jit_solution(3301209582469114586)
XLA Ops:
  0.6 71.3 %shard_map.86.result = bf16[2,14,256,256]{3,2,1,0:T(8,128)(2,1)S(1)} custom-call(bf16[14,256,256]{2,1,0:T(8,128)(2,1)} %bitcast.7, bf16[14,256,256]{2,1,0:T(8,128)(2,1)} %bitcast.8, bf16[4,256,256]{2,1,0:T(8,128)(2,1)} %bitcast.11, bf16[4,256,256]{2,1,0:T(8,128)(2,1)} %bitcast.12, bf16[14,4,4,14]{3,2,1,0:T(4,128)(2,1)} %refs_4_.1, s32[4]{0:T(128)} %bitcast.13, ...), custom_call_target="tpu_custom_call" | custom-call | flops 7824474112 | bytes 10485760 | tf_op jit(solution)/shard_map/pallas_call | solution.py:324
  71.9 1.9 %shard_map.87 = (bf16[14,256,256]{2,1,0:T(8,128)(2,1)}, bf16[14,256,256]{2,1,0:T(8,128)(2,1)}) custom-call(bf16[2,14,256,256]{3,2,1,0:T(8,128)(2,1)S(1)} %shard_map.86.result), custom_call_target="tpu_custom_call" | custom-call | tf_op jit(solution)/shard_map/pallas_call | solution.py:355

commit v6 on v5

--- a/solution.py
+++ b/solution.py
@@ -208,7 +208,7 @@
                     part = site[side, :, q * UNIT_ROWS : (q + 1) * UNIT_ROWS, :]
                     turned[side, q] = part.reshape(4 * UNIT_ROWS, slot).astype(F32).T.astype(BF)
 
-    def unit(side, q):
+    def unit(side, q, final):
         span = pl.ds(pl.multiple_of(q * UNIT_ROWS, UNIT_ROWS), UNIT_ROWS)
         for s in range(4):
             held = env[side, (s + 1) // 2, :, span, :].reshape(width * UNIT_ROWS, slot)
@@ -232,8 +232,10 @@
         for v in range(width):
             held = mixed[v].reshape(4 * UNIT_ROWS, slot)
             value = total[side, v] + jnp.dot(turned[side, q], held, preferred_element_type=F32)
-            total[side, v] = value
-            result[side, v] = value.astype(BF)
+            if final:
+                result[side, v] = value.astype(BF)
+            else:
+                total[side, v] = value
 
     def got(side):
         return jnp.where(side == 0, i, chains - 1 - i) > 0
@@ -253,7 +255,7 @@
             @pl.when(got(side) & (c >= 2))
             def _():
                 d_wait(side, c - 2)
-                unit(side, c - 2)
+                unit(side, c - 2, False)
 
             @pl.when((c >= 1) & (c <= steps) & (side == 0))
             def _():
@@ -269,7 +271,17 @@
 
         return carry
 
-    lax.fori_loop(0, steps + 2, step, 0)
+    lax.fori_loop(0, steps + 1, step, 0)
+
+    def finish(side, carry):
+        @pl.when(got(side))
+        def _():
+            d_wait(side, steps - 1)
+            unit(side, units - 1, True)
+
+        return carry
+
+    lax.fori_loop(0, 2, finish, 0)
 
     def settle(c, carry):
         for side in range(2):

time: 73.9 us -> 73.9 us (level)
  no operation moved by 1% of the time
where the time goes in v6:
time: 73.9 us; the launch traced here: 73.7 us
  Pallas kernels  73.1 us (99%)
    pallas_call x1, Pallas kernels, body(): pl.pallas_call(run, out_shape=pltpu.VMEM((2, width, slot, slot), BF), in_...  71.2 us
    pallas_call x1, Pallas kernels, body(): pl.pallas_call(write_out, out_shape=[jax.ShapeDtypeStruct((width, slot, s...  1.87 us

profile of v6, /device:TPU:128, one launch (start us, length us, event | category | flops | bytes accessed | tf_op | source)
XLA Modules:
  0.0 73.7 jit_solution(5726808449842299387)
XLA Ops:
  0.6 71.2 %shard_map.86.result = bf16[2,14,256,256]{3,2,1,0:T(8,128)(2,1)S(1)} custom-call(bf16[14,256,256]{2,1,0:T(8,128)(2,1)} %bitcast.7, bf16[14,256,256]{2,1,0:T(8,128)(2,1)} %bitcast.8, bf16[4,256,256]{2,1,0:T(8,128)(2,1)} %bitcast.11, bf16[4,256,256]{2,1,0:T(8,128)(2,1)} %bitcast.12, bf16[14,4,4,14]{3,2,1,0:T(4,128)(2,1)} %refs_4_.1, s32[4]{0:T(128)} %bitcast.13, ...), custom_call_target="tpu_custom_call" | custom-call | flops 7824474112 | bytes 10485760 | tf_op jit(solution)/shard_map/pallas_call | solution.py:336
  71.9 1.9 %shard_map.87 = (bf16[14,256,256]{2,1,0:T(8,128)(2,1)}, bf16[14,256,256]{2,1,0:T(8,128)(2,1)}) custom-call(bf16[2,14,256,256]{3,2,1,0:T(8,128)(2,1)S(1)} %shard_map.86.result), custom_call_target="tpu_custom_call" | custom-call | tf_op jit(solution)/shard_map/pallas_call | solution.py:367
